TPU v7x, 32 devices: a whole 2x2x4 slice. The times are simulated.
32 devices in a mesh: cuts: 4 (over y, core), stem: 8 (over z, x).
Axes of the slice: x: 2, y: 2, z: 4, core: 2. Of those that a mesh axis runs over, the one named last changes fastest.
Arguments:
- stem_tensor: float32 [2048, 1024], P(('cuts', 'stem')), parts along dimension 0, may hold values from -0.25 to 0.25
- stem_cotangent: float32 [2048, 1024], P(('cuts', 'stem')), parts along dimension 0, may hold values from -6 to 6
- branch_tensor: bfloat16 [1024, 1024], P('stem'), may hold values from -0.1875 to 0.1875
- bit_order: int32 [16], replicated, may hold values from 0 to 15, each once
Outputs:
- stem_grad: float32 [2048, 1024], P(('cuts', 'stem')), parts along dimension 0
- branch_grad: float32 [4096, 1024], P(('cuts', 'stem')), parts along dimension 0
There are 4 independent parts, one for each index of `cuts`. A program takes and returns all parts, laid end to end along the dimension named above; an argument that names none is the same for every part. Nothing has to cross between parts.
Inputs may be any that keep to these rules, and one draw needn't show every extreme that they name: `bit_order`: a permutation of the 16 local index bit positions.
All inputs are finite; a program needn't handle non-finite values.
Results may differ from a plain program's by a relative error of at most 0.0003.
Values may be sent and summed in bfloat16 or wider, within the bound.
A program may use at most 64 MiB of HBM per device.

v0:
```python
import jax
import jax.numpy as jnp
from jax import lax
from jax.sharding import PartitionSpec as P


def bit_tables(bit_order, local_bits, dev_bits):
    local_size = 2**local_bits
    positions = jnp.arange(local_size, dtype=jnp.int32)
    forward = jnp.zeros((local_size,), jnp.int32)
    backward = jnp.zeros((local_size,), jnp.int32)
    for order_pos in range(local_bits):
        if order_pos < dev_bits:
            target_bit = dev_bits - 1 - order_pos
        else:
            target_bit = dev_bits + local_bits - 1 - order_pos
        source = bit_order[order_pos]
        forward = forward + jnp.left_shift(jnp.right_shift(positions, source) & 1, target_bit)
        backward = backward + jnp.left_shift(jnp.right_shift(positions, target_bit) & 1, source)
    return (forward, backward)


def cross_bits(operands):
    return (lax.all_to_all(operands[0], "stem", split_axis=1, concat_axis=1, tiled=True),)


def per_device(stem_tensor, stem_cotangent, branch_tensor, bit_order):
    members = lax.axis_size("stem")
    dev_bits = members.bit_length() - 1
    row_count, width = stem_tensor.shape
    local_size = row_count * width
    local_bits = local_size.bit_length() - 1
    free_size = local_size // members
    forward, backward = bit_tables(bit_order, local_bits, dev_bits)
    arranged = jnp.take(stem_tensor.reshape(local_size), backward).reshape(free_size, members)
    gathered = lax.all_gather(branch_tensor, "stem", axis=0, tiled=True)
    adjoint = lax.dot_general(
        stem_cotangent,
        gathered.astype(jnp.float32),
        (((1,), (1,)), ((), ())),
        precision=lax.Precision.HIGHEST,
        preferred_element_type=jnp.float32,
    )
    (moved,) = cross_bits((arranged,))
    (returned,) = cross_bits((adjoint.reshape(free_size, members),))
    perm_stem = moved.reshape(row_count, width)
    branch_term = lax.dot_general(
        perm_stem,
        stem_cotangent,
        (((0,), (0,)), ((), ())),
        precision=lax.Precision.HIGHEST,
        preferred_element_type=jnp.float32,
    )
    branch_grad = lax.psum_scatter(branch_term, "stem", scatter_dimension=0, tiled=True)
    stem_grad = jnp.take(returned.reshape(local_size), forward).reshape(row_count, width)
    return (stem_grad, branch_grad)


def solution(mesh):
    placed = (P(("cuts", "stem"), None), P(("cuts", "stem"), None), P("stem", None), P())
    return jax.shard_map(
        per_device,
        mesh=mesh,
        in_specs=placed,
        out_specs=(P(("cuts", "stem"), None), P(("cuts", "stem"), None)),
        check_vma=False,
    )
```

profile of v0, /device:TPU:0, one launch (start us, length us, event | category | flops | bytes accessed | tf_op | source)
XLA Modules:
  0.0 847.5 jit_solution(13714084007219988418)
XLA Ops:
  7.2 0.0 copy-start
  7.2 0.0 all-gather.2.cloned.1.call-start
  7.2 0.7 all-gather.2.cloned.1.call-update
  7.9 0.0 reduce-scatter.2.cloned.1.call-start
  8.0 1.0 copy.10
  9.0 1.9 fusion
  10.9 10.5 %broadcast_clamp_fusion = s32[65536]{0:T(1024)S(1)} fusion(s32[]{:T(128)} %bitcast.15, s32[]{:T(128)} %bitcast.14, s32[]{:T(128)} %bitcast.13, s32[]{:T(128)} %bitcast.12, s32[]{:T(128)} %bitcast.11, s32[]{:T(128)} %bitcast.10, s32[]{:T(128)} %bitcast.9, s32[]{:T(128)} %bitcast.8, s32[]{:T(128)} %bitcast.7, s32[]{:T(128)} %bitcast.6, s32[]{:T(128)} %bitcast.5, ...), kind=kLoop, calls=%fused_computation.6 | loop fusion | flops 4390912 | bytes 262208 | tf_op gather
  21.4 362.7 %gather_fusion.1 = f32[65536]{0:T(1024)S(1)} fusion(f32[65536]{0:T(1024)S(1)} %bitcast.26, s32[65536]{0:T(1024)S(1)} %broadcast_clamp_fusion), kind=kCustom, calls=%fused_computation.1.clone | custom fusion | bytes 786432 | tf_op jit(solution)/shard_map/jit(_take)/gather | solution.py:35
  384.1 10.5 %and_select_fusion = f32[65536]{0:T(1024)S(1)} fusion(f32[65536]{0:T(1024)S(1)} %gather_fusion.1, s32[]{:T(128)} %bitcast.15, s32[]{:T(128)} %bitcast.14, s32[]{:T(128)} %bitcast.13, s32[]{:T(128)} %bitcast.12, s32[]{:T(128)} %bitcast.11, s32[]{:T(128)} %bitcast.10, s32[]{:T(128)} %bitcast.9, s32[]{:T(128)} %bitcast.8, s32[]{:T(128)} %bitcast.7, s32[]{:T(128)} %bitcast.6, ...), kind=kLoop, calls=%fused_computation.4 | loop fusion | flops 4587520 | bytes 524352 | tf_op jit(solution)/shard_map/jit(_take)/select_n | solution.py:35
  394.6 3.6 all_to_all.14
  398.2 2.8 copy.8
  401.0 16.0 %all_to_all.18 = f32[8192,8,1]{0,2,1:T(1,128)S(1)} all-to-all(f32[8192,8,1]{0,2,1:T(1,128)S(1)} %copy.8), channel_id=1, replica_groups=mesh['cuts'=4,'stem'=8] {'stem'}, dimensions={1} | all-to-all | bytes 524288 | tf_op jit(solution)/shard_map/all_to_all | solution.py:24
  417.0 2.6 copy.9
  419.5 4.0 reshape.34
  423.5 0.0 copy-done
  423.5 5.0 fusion.2
  428.6 0.0 reduce-scatter.2.cloned.1.call-update
  428.6 0.0 all-gather.2.cloned.1.call-done
  428.6 3.6 fusion.1
  432.3 3.7 all_to_all.12
  435.9 3.5 copy.6
  439.4 4.0 all-to-all-start
  443.4 10.5 %broadcast_clamp_fusion.1 = s32[65536]{0:T(1024)S(1)} fusion(s32[]{:T(128)} %bitcast.15, s32[]{:T(128)} %bitcast.14, s32[]{:T(128)} %bitcast.13, s32[]{:T(128)} %bitcast.12, s32[]{:T(128)} %bitcast.11, s32[]{:T(128)} %bitcast.10, s32[]{:T(128)} %bitcast.9, s32[]{:T(128)} %bitcast.8, s32[]{:T(128)} %bitcast.7, s32[]{:T(128)} %bitcast.6, s32[]{:T(128)} %bitcast.5, ...), kind=kLoop, calls=%fused_computation.7 | loop fusion | flops 4390912 | bytes 262208 | tf_op gather
  453.8 6.6 all-to-all-done
  460.4 2.7 copy.7
  463.1 3.7 reshape.31
  466.8 362.7 %gather_fusion = f32[65536]{0:T(1024)S(1)} fusion(f32[65536]{0:T(1024)S(1)} %reshape.31, s32[65536]{0:T(1024)S(1)} %broadcast_clamp_fusion.1), kind=kCustom, calls=%fused_computation.clone | custom fusion | bytes 786432 | tf_op jit(solution)/shard_map/jit(_take)/gather | solution.py:55
  829.5 10.5 %and_select_fusion.1 = f32[65536]{0:T(1024)S(1)} fusion(f32[65536]{0:T(1024)S(1)} %gather_fusion, s32[]{:T(128)} %bitcast.15, s32[]{:T(128)} %bitcast.14, s32[]{:T(128)} %bitcast.13, s32[]{:T(128)} %bitcast.12, s32[]{:T(128)} %bitcast.11, s32[]{:T(128)} %bitcast.10, s32[]{:T(128)} %bitcast.9, s32[]{:T(128)} %bitcast.8, s32[]{:T(128)} %bitcast.7, s32[]{:T(128)} %bitcast.6, ...), kind=kLoop, calls=%fused_computation.5 | loop fusion | flops 4587520 | bytes 524352 | tf_op jit(solution)/shard_map/jit(_take)/select_n | solution.py:55
  840.0 0.7 reshape.32
  840.7 0.0 reduce-scatter.2.cloned.1.call-done
Async XLA Ops:
  7.2 416.4 %copy-start = (f32[64,1024]{1,0:T(8,128)S(1)}, f32[64,1024]{1,0:T(8,128)}, u32[]{:S(2)}) copy-start(f32[64,1024]{1,0:T(8,128)} %param.7) | copy-start | bytes 786436
  7.2 421.5 %all-gather.2.cloned.1.call-start = ((), (), s32[]{:S(2)}) async-start(), calls=%async_computation.3 | async-start | bytes 2359296 | tf_op jit(solution)/shard_map/all_gather | solution.py:36
  7.9 832.8 %reduce-scatter.2.cloned.1.call-start = ((), (), s32[]{:S(2)}) async-start(), calls=%async_computation.4 | async-start | bytes 4718592 | tf_op jit(solution)/shard_map/reduce_scatter | solution.py:54
  439.4 21.0 %all-to-all-start = ((f32[8192,8,1]{0,2,1:T(1,128)}), f32[8192,8,1]{0,2,1:T(1,128)S(1)}, u32[]{:S(2)}, u32[]{:S(2)}) async-start(f32[8192,8,1]{0,2,1:T(1,128)} %copy.6), calls=%async_computation | async-start | bytes 524288 | tf_op jit(solution)/shard_map/all_to_all | solution.py:24
Sparse Core Ops, SparseCore 0:
  10.1 51.9 all-gather.1
  428.7 91.8 reduce-scatter.1
where the time goes:
time: 848 us
  local copies, waits for them, and re-layouts  756 us (89%)
  other arithmetic  41.9 us (5%)
  blocking collectives  16 us (2%)
  between operations  14.1 us (2%)
  matrix products  8.66 us (1%)
    gather x1, local copies, waits for them, and re-layouts, per_device(): jnp.take(stem_tensor.reshape(local_size), backward)  363 us
    gather x1, local copies, waits for them, and re-layouts, per_device(): jnp.take(returned.reshape(local_size), forward).reshape(row_count, width)  363 us
    gather x2, other arithmetic  20.9 us
    all_to_all x6, local copies, waits for them, and re-layouts, cross_bits(): lax.all_to_all(operands[0], 'stem', split_axis=1, concat_axis=1, tiled=True)  18.8 us
  transfers between devices with their start and end apart: 3, of which 1 were waited for; matrix products, arithmetic and copies ran while one was open for 94% of the time, Pallas kernels for 0%

commit v1 on v0

--- a/solution.py
+++ b/solution.py
@@ -21,7 +21,14 @@
 
 
 def cross_bits(operands):
-    return (lax.all_to_all(operands[0], "stem", split_axis=1, concat_axis=1, tiled=True),)
+    return (
+        jnp.concatenate(
+            lax.all_to_all(
+                jnp.stack(jnp.split(operands[0], lax.axis_size("stem"), axis=1)), "stem", 0, 0
+            ),
+            axis=1,
+        ),
+    )
 
 
 def per_device(stem_tensor, stem_cotangent, branch_tensor, bit_order):

time: 848 us -> 892 us (1.052)
  local copies, waits for them, and re-layouts: 756 us -> 806 us
  blocking collectives: 16 us -> 28.9 us
  other arithmetic: 41.9 us -> 32.3 us
    split x0 -> x2, local copies, waits for them, and re-layouts: none -> 56.8 us  [cross_bits(): jnp.split(operands[0], lax.axis_size('stem'), axis=1)]
    all_to_all x6 -> x0, local copies, waits for them, and re-layouts: 18.8 us -> none  [cross_bits(): lax.all_to_all(operands[0], 'stem', split_axis=1, concat_axis=1, tiled=True)]
    all_to_all x1 -> x2, blocking collectives: 16 us -> 28.9 us  [cross_bits(): lax.all_to_all(jnp.stack(jnp.split(operands[0], lax.axis_size('stem'), ax...]
    gather x2 -> x1, other arithmetic: 20.9 us -> 11.2 us
  transfers between devices with their start and end apart: 3 -> 2, of which waited for: 1 -> 0; matrix products, arithmetic and copies ran while one was open for 94% -> 95% of each run, Pallas kernels for 0% -> 0%
where the time goes in v1:
time: 892 us; the launch traced here: 891 us
  local copies, waits for them, and re-layouts  806 us (90%)
  other arithmetic  32.3 us (4%)
  blocking collectives  28.9 us (3%)
  between operations  14.2 us (2%)
    gather x1, local copies, waits for them, and re-layouts, per_device(): jnp.take(stem_tensor.reshape(local_size), backward)  363 us
    gather x1, local copies, waits for them, and re-layouts, per_device(): jnp.take(returned.reshape(local_size), forward).reshape(row_count, width)  363 us
    split x2, local copies, waits for them, and re-layouts, cross_bits(): jnp.split(operands[0], lax.axis_size('stem'), axis=1)  56.8 us
    all_to_all x2, blocking collectives, cross_bits(): lax.all_to_all(jnp.stack(jnp.split(operands[0], lax.axis_size('stem'), ax...  28.9 us
  transfers between devices with their start and end apart: 2, of which 0 were waited for; matrix products, arithmetic and copies ran while one was open for 95% of the time, Pallas kernels for 0%

profile of v1, /device:TPU:0, one launch (start us, length us, event | category | flops | bytes accessed | tf_op | source)
XLA Modules:
  0.0 891.0 jit_solution(4102315403626589164)
XLA Ops:
  7.2 0.0 copy-start
  7.2 0.0 all-gather.2.cloned.1.call-start
  7.2 0.7 all-gather.2.cloned.1.call-update
  7.9 0.0 reduce-scatter.2.cloned.1.call-start
  8.0 2.0 fusion
  9.9 1.0 copy.32
  10.9 11.2 %broadcast_clamp_fusion = (s32[65536]{0:T(1024)S(1)}, s32[65536]{0:T(1024)S(1)}) fusion(s32[]{:T(128)} %bitcast.15, s32[]{:T(128)} %bitcast.14, s32[]{:T(128)} %bitcast.13, s32[]{:T(128)} %bitcast.12, s32[]{:T(128)} %bitcast.11, s32[]{:T(128)} %bitcast.10, s32[]{:T(128)} %bitcast.9, s32[]{:T(128)} %bitcast.8, s32[]{:T(128)} %bitcast.7, s32[]{:T(128)} %bitcast.6, ...), kind=kLoop, calls=%fused_computation.22 | loop fusion | flops 8781824 | bytes 524352 | tf_op gather
  22.1 362.7 %gather_fusion.1 = f32[65536]{0:T(1024)S(1)} fusion(f32[65536]{0:T(1024)S(1)} %bitcast.44, s32[65536]{0:T(1024)S(1)} %get-tuple-element.35), kind=kCustom, calls=%fused_computation.1.clone | custom fusion | bytes 786432 | tf_op jit(solution)/shard_map/jit(_take)/gather | solution.py:42
  384.8 10.6 %and_select_fusion = f32[65536]{0:T(1024)S(1)} fusion(f32[65536]{0:T(1024)S(1)} %gather_fusion.1, s32[]{:T(128)} %bitcast.15, s32[]{:T(128)} %bitcast.14, s32[]{:T(128)} %bitcast.13, s32[]{:T(128)} %bitcast.12, s32[]{:T(128)} %bitcast.11, s32[]{:T(128)} %bitcast.10, s32[]{:T(128)} %bitcast.9, s32[]{:T(128)} %bitcast.8, s32[]{:T(128)} %bitcast.7, s32[]{:T(128)} %bitcast.6, ...), kind=kLoop, calls=%fused_computation.20 | loop fusion | flops 4587520 | bytes 524352 | tf_op jit(solution)/shard_map/jit(_take)/select_n | solution.py:42
  395.4 3.6 reshape.31
  399.0 28.3 %slice_reduce_fusion = (f32[8192]{0:T(1024)S(1)}, f32[8192]{0:T(1024)S(1)}, f32[8192]{0:T(1024)S(1)}, f32[8192]{0:T(1024)S(1)}, f32[8192]{0:T(1024)S(1)}, /*inde...) fusion(f32[8192,8]{1,0:T(8,128)} %reshape.31), kind=kLoop, calls=%fused_computation.2 | loop fusion | bytes 524288 | tf_op jit(solution)/shard_map/split | solution.py:27
  427.4 16.0 %all_to_all.10 = f32[8,8192,1]{1,2,0:T(1,128)S(1)} all-to-all(f32[8,8192,1]{1,2,0:T(1,128)S(1)} %constant_dynamic-update-slice_fusion.8), channel_id=1, replica_groups=mesh['cuts'=4,'stem'=8] {'stem'}, dimensions={0} | all-to-all | bytes 524288 | tf_op jit(solution)/shard_map/all_to_all | solution.py:26
  443.4 2.6 copy.31
  446.0 4.0 reshape_reshape.7
  450.0 0.0 copy-done
  450.0 5.1 fusion.2
  455.0 0.0 reduce-scatter.2.cloned.1.call-update
  455.1 0.0 all-gather.2.cloned.1.call-done
  455.1 3.6 fusion.1
  458.7 3.7 reshape.27
  462.4 28.4 %slice_reduce_fusion.8 = (f32[8192]{0:T(1024)S(1)}, f32[8192]{0:T(1024)S(1)}, f32[8192]{0:T(1024)S(1)}, f32[8192]{0:T(1024)S(1)}, f32[8192]{0:T(1024)S(1)}, /*in...) fusion(f32[8192,8]{1,0:T(8,128)} %reshape.27), kind=kLoop, calls=%fused_computation.10 | loop fusion | bytes 524288 | tf_op jit(solution)/shard_map/split | solution.py:27
  490.9 12.9 %all_to_all.11 = f32[8,8192,1]{1,2,0:T(1,128)S(1)} all-to-all(f32[8,8192,1]{1,2,0:T(1,128)S(1)} %constant_dynamic-update-slice_fusion), channel_id=1, replica_groups=mesh['cuts'=4,'stem'=8] {'stem'}, dimensions={0} | all-to-all | bytes 524288 | tf_op jit(solution)/shard_map/all_to_all | solution.py:26
  503.8 2.6 copy.30
  506.5 3.7 reshape_reshape.6
  510.2 362.7 %gather_fusion = f32[65536]{0:T(1024)S(1)} fusion(f32[65536]{0:T(1024)S(1)} %reshape_reshape.6, s32[65536]{0:T(1024)S(1)} %get-tuple-element.36), kind=kCustom, calls=%fused_computation.clone | custom fusion | bytes 786432 | tf_op jit(solution)/shard_map/jit(_take)/gather | solution.py:62
  872.9 10.6 %and_select_fusion.1 = f32[65536]{0:T(1024)S(1)} fusion(f32[65536]{0:T(1024)S(1)} %gather_fusion, s32[]{:T(128)} %bitcast.15, s32[]{:T(128)} %bitcast.14, s32[]{:T(128)} %bitcast.13, s32[]{:T(128)} %bitcast.12, s32[]{:T(128)} %bitcast.11, s32[]{:T(128)} %bitcast.10, s32[]{:T(128)} %bitcast.9, s32[]{:T(128)} %bitcast.8, s32[]{:T(128)} %bitcast.7, s32[]{:T(128)} %bitcast.6, ...), kind=kLoop, calls=%fused_computation.21 | loop fusion | flops 4587520 | bytes 524352 | tf_op jit(solution)/shard_map/jit(_take)/select_n | solution.py:62
  883.5 0.7 reshape.29
  884.2 0.0 reduce-scatter.2.cloned.1.call-done
  (16 shorter events, 0.2 us)
Async XLA Ops:
  7.2 442.8 %copy-start = (f32[64,1024]{1,0:T(8,128)S(1)}, f32[64,1024]{1,0:T(8,128)}, u32[]{:S(2)}) copy-start(f32[64,1024]{1,0:T(8,128)} %param.7) | copy-start | bytes 786436
  7.2 447.9 %all-gather.2.cloned.1.call-start = ((), (), s32[]{:S(2)}) async-start(), calls=%async_computation.3 | async-start | bytes 2359296 | tf_op jit(solution)/shard_map/all_gather | solution.py:43
  7.9 876.3 %reduce-scatter.2.cloned.1.call-start = ((), (), s32[]{:S(2)}) async-start(), calls=%async_computation.4 | async-start | bytes 4718592 | tf_op jit(solution)/shard_map/reduce_scatter | solution.py:61
Sparse Core Ops, SparseCore 0:
  10.1 52.1 all-gather.1
  455.2 89.7 reduce-scatter.1
